TPU v7x, 32 devices: a whole 2x2x4 slice. The times are simulated.
32 devices in a mesh: groups: 2 (over y), row: 4 (over z), col: 2 (over core), seq: 2 (over x).
Axes of the slice: x: 2, y: 2, z: 4, core: 2. Of those that a mesh axis runs over, the one named last changes fastest.
Arguments:
- alignment: bfloat16 [512, 64, 256], P(('groups', 'seq'), ('row', 'col')), parts along dimension 0, may hold values from -16 to 16
- alignment_mask: bfloat16 [512, 64], P(('groups', 'seq'), ('row', 'col')), parts along dimension 0, may hold values from 0 to 1
- norm_gain: float32 [256], replicated, may hold values from 0.1 to 1.9
- norm_bias: float32 [256], replicated, may hold values from -3 to 3
- left_weight: bfloat16 [256, 32], replicated, may hold values from -0.375 to 0.375
- left_bias: float32 [32], replicated, may hold values from -3 to 3
- right_weight: bfloat16 [256, 32], replicated, may hold values from -0.375 to 0.375
- right_bias: float32 [32], replicated, may hold values from -3 to 3
- out_weight: bfloat16 [1024, 128], replicated, may hold values from -0.1875 to 0.1875
- pair_state: bfloat16 [128, 64, 128], P(('groups', 'row'), ('col', 'seq')), parts along dimension 0, may hold values from -6 to 6
Outputs:
- pair_out: bfloat16 [128, 64, 128], P(('groups', 'row'), ('col', 'seq')), parts along dimension 0
There are 2 independent parts, one for each index of `groups`. A program takes and returns all parts, laid end to end along the dimension named above; an argument that names none is the same for every part. Nothing has to cross between parts.
All inputs are finite; a program needn't handle non-finite values.
Results may differ from a plain program's by a relative error of at most 0.0034.
Values may be sent and summed in bfloat16 or wider, within the bound.
A program may use at most 64 MiB of HBM per device.

v0:
```python
import jax
import jax.numpy as jnp
from jax import lax
from jax.sharding import PartitionSpec as P


def normalize(alignment, norm_gain, norm_bias):
    values = alignment.astype(jnp.float32)
    center = jnp.mean(values, axis=-1, keepdims=True)
    spread = jnp.mean(jnp.square(values - center), axis=-1, keepdims=True)
    return ((values - center) * lax.rsqrt(spread + 1e-05) * norm_gain + norm_bias).astype(
        jnp.bfloat16
    )


def project(normed, mask_float, weight, shift):
    seq_count, shard_size, channels = normed.shape
    flat_rows = normed.reshape(seq_count * shard_size, channels)
    product = jnp.dot(flat_rows, weight, preferred_element_type=jnp.float32).reshape(
        seq_count, shard_size, weight.shape[1]
    )
    return ((product + shift) * mask_float[:, :, None]).astype(jnp.bfloat16)


def numerate(left_rows, right_cols, weight_flat):
    seq_count, row_total, channels = left_rows.shape
    col_total = right_cols.shape[1]
    pair_chans = weight_flat.shape[1]
    block_rows = 4
    block_count = row_total // block_rows
    left_blocks = left_rows.reshape(seq_count, block_count, block_rows, channels).transpose(
        1, 0, 2, 3
    )

    def block_step(left_block):
        outer = jnp.einsum(
            "sic,sje->ijce", left_block, right_cols, preferred_element_type=jnp.float32
        )
        outer = outer.reshape(block_rows * col_total, channels * channels)
        return jnp.dot(
            outer, weight_flat, precision=lax.Precision.HIGHEST, preferred_element_type=jnp.float32
        ).reshape(block_rows, col_total, pair_chans)

    results = lax.map(block_step, left_blocks)
    return results.reshape(row_total, col_total, pair_chans)


def on_device(
    alignment,
    alignment_mask,
    norm_gain,
    norm_bias,
    left_weight,
    left_bias,
    right_weight,
    right_bias,
    out_weight,
    pair_state,
):
    mask_float = alignment_mask.astype(jnp.float32)
    normed = normalize(alignment, norm_gain, norm_bias)
    left_local = project(normed, mask_float, left_weight, left_bias)
    right_local = project(normed, mask_float, right_weight, right_bias)
    left_rows, left_present = (
        lax.all_gather(left_local, "col", axis=1, tiled=True),
        lax.all_gather(alignment_mask, "col", axis=1, tiled=True),
    )
    row_count = lax.axis_size("row")
    column_index = lax.axis_index("col")
    seq_count, shard_size, channels = right_local.shape
    block_width = shard_size * row_count
    every_row, every_mask = (
        lax.all_gather(right_local, ("row", "col"), axis=1, tiled=True),
        lax.all_gather(alignment_mask, ("row", "col"), axis=1, tiled=True),
    )
    right_cols = lax.dynamic_slice_in_dim(every_row, column_index * block_width, block_width, 1)
    right_mask = lax.dynamic_slice_in_dim(every_mask, column_index * block_width, block_width, 1)
    weight_flat = out_weight.astype(jnp.float32)
    numer_part = numerate(left_rows, right_cols, weight_flat)
    count_part = jnp.einsum(
        "si,sj->ij", left_present, right_mask, preferred_element_type=jnp.float32
    )
    numerator, counts = (
        lax.psum_scatter(numer_part, "seq", scatter_dimension=1, tiled=True),
        lax.psum_scatter(count_part, "seq", scatter_dimension=1, tiled=True),
    )
    return (pair_state.astype(jnp.float32) + numerator / (counts[:, :, None] + 0.001)).astype(
        jnp.bfloat16
    )


def solution(mesh):
    in_specs = (
        P(("groups", "seq"), ("row", "col"), None),
        P(("groups", "seq"), ("row", "col")),
        P(),
        P(),
        P(),
        P(),
        P(),
        P(),
        P(),
        P(("groups", "row"), ("col", "seq"), None),
    )
    out_specs = P(("groups", "row"), ("col", "seq"), None)
    return jax.shard_map(
        on_device, mesh=mesh, in_specs=in_specs, out_specs=out_specs, check_vma=False
    )
```

profile of v0, /device:TPU:1, one launch (start us, length us, event | category | flops | bytes accessed | tf_op | source)
XLA Modules:
  0.0 77.3 jit_solution(5835595009026654709)
XLA Ops:
  6.5 14.5 %all_gather.14 = bf16[128,64]{0,1:T(8,128)(2,1)S(1)} all-gather(bf16[128,8]{0,1:T(8,128)(2,1)} %param.13), channel_id=1, replica_groups=mesh['groups'=2,'row'=4,'col'=2,'seq'=2] {'row','col'}, dimensions={1}, use_global_device_ids=true | all-gather | bytes 18432 | tf_op jit(solution)/shard_map/all_gather | solution.py:74
  21.0 1.9 %all_gather.15 = bf16[128,16]{0,1:T(8,128)(2,1)S(1)} all-gather(bf16[128,8]{0,1:T(8,128)(2,1)} %param.13), channel_id=1, replica_groups=mesh['groups'=2,'row'=4,'col'=2,'seq'=2] {'col'}, dimensions={1}, use_global_device_ids=true | all-gather | bytes 6144 | tf_op jit(solution)/shard_map/all_gather | solution.py:66
  22.9 0.1 convolution_bitcast_fusion.2
  23.1 0.7 copy.20
  23.8 0.0 reduce-scatter.5.cloned.1.call-start
  23.8 0.7 convert_element_type.27
  24.5 1.3 %convert_reduce_fusion = f32[128,8]{1,0:T(8,128)S(1)} fusion(bf16[128,8,256]{2,1,0:T(8,128)(2,1)} %param.12), kind=kLoop, calls=%fused_computation.9 | loop fusion | flops 523264 | bytes 528384 | tf_op jit(solution)/shard_map/reduce_sum | solution.py:9
  25.8 1.4 %fusion.8 = f32[128,8]{1,0:T(8,128)S(1)} fusion(bf16[128,8,256]{2,1,0:T(8,128)(2,1)} %param.12, f32[128,8]{1,0:T(8,128)S(1)} %broadcast_multiply_fusion), kind=kLoop, calls=%fused_computation.13 | loop fusion | flops 1047552 | bytes 532480 | tf_op jit(solution)/shard_map/reduce_sum | solution.py:10
  27.2 1.5 %fusion.14 = f32[128,8,32]{2,1,0:T(8,128)S(1)} fusion(bf16[128,8,256]{2,1,0:T(8,128)(2,1)} %param.12, f32[256]{0:T(256)} %param.15, f32[256]{0:T(256)} %param.14, f32[128,8]{1,0:T(8,128)S(1)} %add_rsqrt_fusion, f32[128,8]{1,0:T(8,128)S(1)} %broadcast_multiply_fusion, bf16[256,32]{0,1:T(8,128)(2,1)S(1)} %copy-done), kind=kOutput, calls=%fused_computation.18 | convolution fusion | flops 18350080 | bytes 681984 | tf_op jit(solution)/shard_map/dot_general | solution.py:19
  28.8 0.2 copy.17
  29.0 0.5 fusion.12
  29.5 0.2 copy.19
  29.7 0.1 multiply_convert_fusion
  29.8 14.8 %all_gather.13 = bf16[128,64,32]{0,2,1:T(8,128)(2,1)S(1)} all-gather(bf16[128,8,32]{0,2,1:T(8,128)(2,1)S(1)} %get-tuple-element.43), channel_id=1, replica_groups=mesh['groups'=2,'row'=4,'col'=2,'seq'=2] {'row','col'}, dimensions={1}, use_global_device_ids=true | all-gather | bytes 589824 | tf_op jit(solution)/shard_map/all_gather | solution.py:73
  44.6 1.9 %all_gather.12 = bf16[128,16,32]{0,2,1:T(8,128)(2,1)S(1)} all-gather(bf16[128,8,32]{0,2,1:T(8,128)(2,1)S(1)} %get-tuple-element.44), channel_id=1, replica_groups=mesh['groups'=2,'row'=4,'col'=2,'seq'=2] {'col'}, dimensions={1}, use_global_device_ids=true | all-gather | bytes 196608 | tf_op jit(solution)/shard_map/all_gather | solution.py:65
  46.5 11.1 %while.10 = (s32[]{:T(128)}, f32[4,4,32,128]{3,2,1,0:T(8,128)}, bf16[4,128,4,32]{1,3,2,0:T(8,128)(2,1)S(1)}, bf16[128,32,32]{0,2,1:T(8,128)(2,1)S(1)}, f32[1024,128]{1,0:T(8,128)S(1)}, /*index=5*/s32[]{:T(128)}) while((s32[]{:T(128)}, f32[4,4,32,128]{3,2,1,0:T(8,128)}, bf16[4,128,4,32]{1,3,2,0:T(8,128)(2,1)S(1)}, ...), condition=%wide.region_3.4_spmd, body=%wide.region_2.3_spmd.sunk | while | flops 234881024 | bytes 2982473 | solution.py:44
  46.5 0.5 convolution_bitcast_fusion.4
  47.1 1.0 %reshape.53 = f32[4,32,1024]{2,1,0:T(8,128)S(1)} reshape(f32[4,32,32,32]{3,2,1,0:T(8,128)S(1)} %convolution_bitcast_fusion.4) | data formatting | bytes 1048576 | tf_op jit(solution)/shard_map/reshape.20
  48.0 1.3 %fusion.31 = f32[4,4,32,128]{3,2,1,0:T(8,128)} fusion(f32[4,4,32,128]{3,2,1,0:T(8,128)} %get-tuple-element.83, s32[]{:T(128)} %get-tuple-element.82, f32[4,32,1024]{2,1,0:T(8,128)S(1)} %reshape.53, f32[1024,128]{1,0:T(8,128)S(1)} %get-tuple-element.92), kind=kOutput, calls=%fused_computation.2.clone.1 | convolution fusion | flops 201326592 | bytes 1114624 | tf_op jit(solution)/shard_map/while/body/eval_jaxpr/dot_general | solution.py:40
  49.3 0.5 convolution_bitcast_fusion.4
  49.8 1.0 %reshape.53 = f32[4,32,1024]{2,1,0:T(8,128)S(1)} reshape(f32[4,32,32,32]{3,2,1,0:T(8,128)S(1)} %convolution_bitcast_fusion.4) | data formatting | bytes 1048576 | tf_op jit(solution)/shard_map/reshape.20
  50.8 1.3 %fusion.31 = f32[4,4,32,128]{3,2,1,0:T(8,128)} fusion(f32[4,4,32,128]{3,2,1,0:T(8,128)} %get-tuple-element.83, s32[]{:T(128)} %get-tuple-element.82, f32[4,32,1024]{2,1,0:T(8,128)S(1)} %reshape.53, f32[1024,128]{1,0:T(8,128)S(1)} %get-tuple-element.92), kind=kOutput, calls=%fused_computation.2.clone.1 | convolution fusion | flops 201326592 | bytes 1114624 | tf_op jit(solution)/shard_map/while/body/eval_jaxpr/dot_general | solution.py:40
  52.1 0.5 convolution_bitcast_fusion.4
  52.6 1.0 %reshape.53 = f32[4,32,1024]{2,1,0:T(8,128)S(1)} reshape(f32[4,32,32,32]{3,2,1,0:T(8,128)S(1)} %convolution_bitcast_fusion.4) | data formatting | bytes 1048576 | tf_op jit(solution)/shard_map/reshape.20
  53.6 1.3 %fusion.31 = f32[4,4,32,128]{3,2,1,0:T(8,128)} fusion(f32[4,4,32,128]{3,2,1,0:T(8,128)} %get-tuple-element.83, s32[]{:T(128)} %get-tuple-element.82, f32[4,32,1024]{2,1,0:T(8,128)S(1)} %reshape.53, f32[1024,128]{1,0:T(8,128)S(1)} %get-tuple-element.92), kind=kOutput, calls=%fused_computation.2.clone.1 | convolution fusion | flops 201326592 | bytes 1114624 | tf_op jit(solution)/shard_map/while/body/eval_jaxpr/dot_general | solution.py:40
  54.8 0.5 convolution_bitcast_fusion.4
  55.4 1.0 %reshape.53 = f32[4,32,1024]{2,1,0:T(8,128)S(1)} reshape(f32[4,32,32,32]{3,2,1,0:T(8,128)S(1)} %convolution_bitcast_fusion.4) | data formatting | bytes 1048576 | tf_op jit(solution)/shard_map/reshape.20
  56.3 1.3 %fusion.31 = f32[4,4,32,128]{3,2,1,0:T(8,128)} fusion(f32[4,4,32,128]{3,2,1,0:T(8,128)} %get-tuple-element.83, s32[]{:T(128)} %get-tuple-element.82, f32[4,32,1024]{2,1,0:T(8,128)S(1)} %reshape.53, f32[1024,128]{1,0:T(8,128)S(1)} %get-tuple-element.92), kind=kOutput, calls=%fused_computation.2.clone.1 | convolution fusion | flops 201326592 | bytes 1114624 | tf_op jit(solution)/shard_map/while/body/eval_jaxpr/dot_general | solution.py:40
  57.6 0.0 reduce-scatter.7.cloned.1.call-done
  57.7 0.8 copy.21
  58.4 10.4 %reduce-scatter.5.cloned.1.call-done = f32[16,16,128]{2,1,0:T(8,128)} async-done(((f32[16,32,128]{2,1,0:T(8,128)}), f32[16,16,128]{2,1,0:T(8,128)}) %reduce-scatter.5.cloned.1.call-update) | async-done | bytes 131088 | tf_op jit(solution)/shard_map/reduce_scatter | solution.py:84
  68.8 1.6 %add_convert_fusion = bf16[16,16,128]{2,1,0:T(8,128)(2,1)} fusion(f32[16,16,128]{2,1,0:T(8,128)} %reduce-scatter.5.cloned.1.call-done, bf16[16,16,128]{2,1,0:T(8,128)(2,1)} %param.21, f32[16,16]{1,0:T(8,128)S(1)} %broadcast_add_fusion), kind=kLoop, calls=%fused_computation.19 | loop fusion | flops 131072 | bytes 263168 | tf_op jit(solution)/shard_map/convert_element_type | solution.py:87
  (25 shorter events, 0.2 us)
Async XLA Ops:
  6.5 20.7 %copy-start = (bf16[256,32]{0,1:T(8,128)(2,1)S(1)}, bf16[256,32]{0,1:T(8,128)(2,1)}, u32[]{:S(2)}) copy-start(bf16[256,32]{0,1:T(8,128)(2,1)} %param.16) | copy-start | bytes 49156
  6.5 51.1 %reduce-scatter.7.cloned.1.call-start = ((), (), s32[]{:S(2)}) async-start(), calls=%async_computation.3 | async-start | bytes 24576
  23.1 5.9 %copy-start.1 = (bf16[128,8,256]{2,1,0:T(8,128)(2,1)S(1)}, bf16[128,8,256]{2,1,0:T(8,128)(2,1)}, u32[]{:S(2)}) copy-start(bf16[128,8,256]{2,1,0:T(8,128)(2,1)} %param.12) | copy-start | bytes 1572868
  23.1 5.9 %copy-start.5 = (bf16[256,32]{0,1:T(8,128)(2,1)S(1)}, bf16[256,32]{0,1:T(8,128)(2,1)}, u32[]{:S(2)}) copy-start(bf16[256,32]{0,1:T(8,128)(2,1)} %param.18) | copy-start | bytes 49156
  23.1 5.9 %copy-start.6 = (f32[256]{0:T(256)S(1)}, f32[256]{0:T(256)}, u32[]{:S(2)}) copy-start(f32[256]{0:T(256)} %param.15) | copy-start | bytes 3076
  23.1 5.9 %copy-start.7 = (f32[256]{0:T(256)S(1)}, f32[256]{0:T(256)}, u32[]{:S(2)}) copy-start(f32[256]{0:T(256)} %param.14) | copy-start | bytes 3076
  23.8 45.0 %reduce-scatter.5.cloned.1.call-start = ((), (), s32[]{:S(2)}) async-start(), calls=%async_computation.2 | async-start | bytes 393216 | tf_op jit(solution)/shard_map/reduce_scatter | solution.py:84
  28.8 0.9 %copy-start.3 = (f32[32]{0:T(128)S(1)}, f32[32]{0:T(128)}, u32[]{:S(2)}) copy-start(f32[32]{0:T(128)} %param.19) | copy-start | bytes 388
  28.8 0.9 %copy-start.4 = (f32[32]{0:T(128)S(1)}, f32[32]{0:T(128)}, u32[]{:S(2)}) copy-start(f32[32]{0:T(128)} %param.17) | copy-start | bytes 388
  29.0 17.5 %copy-start.2 = (bf16[1024,128]{1,0:T(8,128)(2,1)S(1)}, bf16[1024,128]{1,0:T(8,128)(2,1)}, u32[]{:S(2)}) copy-start(bf16[1024,128]{1,0:T(8,128)(2,1)} %param.20) | copy-start | bytes 786436
Sparse Core Ops, SparseCore 0:
  23.9 8.5 reduce-scatter.6
  57.7 11.0 reduce-scatter.4
where the time goes:
time: 78.3 us; the launch traced here: 77.3 us
  blocking collectives  33 us (42%)
  between operations  13.5 us (17%)
  waiting for transfers between devices  10.4 us (13%)
  matrix products  9.36 us (12%)
  local copies, waits for them, and re-layouts  5.69 us (7%)
  other arithmetic  5.16 us (7%)
    all_gather x1, blocking collectives, on_device(): lax.all_gather(right_local, ('row', 'col'), axis=1, tiled=True)  14.8 us
    all_gather x1, blocking collectives, on_device(): lax.all_gather(alignment_mask, ('row', 'col'), axis=1, tiled=True)  14.5 us
    reduce_scatter x1, waiting for transfers between devices, on_device(): lax.psum_scatter(numer_part, 'seq', scatter_dimension=1, tiled=True)  10.4 us
    dot_general x4, matrix products, block_step(): jnp.dot(outer, weight_flat, precision=lax.Precision.HIGHEST, preferred_el...  5.09 us
    another operation x4, local copies, waits for them, and re-layouts  3.8 us
    dot_general x4, matrix products, block_step(): jnp.einsum('sic,sje->ijce', left_block, right_cols, preferred_element_typ...  2.18 us
    dot_general x2, matrix products, project(): jnp.dot(flat_rows, weight, preferred_element_type=jnp.float32)  1.97 us
    all_gather x1, blocking collectives, on_device(): lax.all_gather(alignment_mask, 'col', axis=1, tiled=True)  1.9 us
  transfers between devices with their start and end apart: 2, of which 1 were waited for; matrix products, arithmetic and copies ran while one was open for 23% of the time, Pallas kernels for 0%

commit v1 on v0

v1 whole, which is shorter than its diff:
```python
import functools

import jax
import jax.numpy as jnp
from jax import lax
from jax.experimental import pallas as pl
from jax.experimental.pallas import tpu as pltpu
from jax.sharding import PartitionSpec as P

MESH = pl.DeviceIdType.MESH
F32 = jnp.float32
BF16 = jnp.bfloat16
ROW_TILE = 16
LANES = 128


def dot_nt(a, b):
    return lax.dot_general(a, b, (((1,), (1,)), ((), ())), preferred_element_type=F32)


def kernel(
    sizes,
    x_ref, mask_ref, gain_ref, bias_ref, wl_ref, bl_ref, wr_ref, br_ref, wout_ref, pair_ref,
    out_ref,
    normed, shuffle, wide, own_right, left_buf, right_buf, spread, big_w, part, part_in,
    count, count_in,
    send_left, recv_left, send_right, recv_right, send_part, recv_part, send_count, recv_count,
):
    n_row, n_col, n_seq = sizes
    seqs, res, chans = x_ref.shape
    ch = wl_ref.shape[1]
    rows_i, cols_j, pair_ch = pair_ref.shape
    block = res * ch
    half = n_row // n_col
    chip_res = res * n_col
    chunks = cols_j // chip_res
    groups = LANES // ch
    ig_count = rows_i // groups
    row, col, seq = lax.axis_index("row"), lax.axis_index("col"), lax.axis_index("seq")
    dest_col = row // half
    my_slot = (row % half) * n_col + col

    barrier = pltpu.get_barrier_semaphore()
    for k in range(1, n_row * n_col):
        flat = (row * n_col + col + k) % (n_row * n_col)
        pl.semaphore_signal(
            barrier, inc=1, device_id={"row": flat // n_col, "col": flat % n_col},
            device_id_type=MESH,
        )
    for k in range(1, n_seq):
        pl.semaphore_signal(
            barrier, inc=1, device_id={"seq": (seq + k) % n_seq}, device_id_type=MESH
        )

    gain, shift = gain_ref[...], bias_ref[...]
    step = 16
    for first in range(0, seqs, step):
        values = x_ref[first : first + step].astype(F32).reshape(step * res, chans)
        center = jnp.mean(values, axis=-1, keepdims=True)
        values = values - center
        var = jnp.mean(values * values, axis=-1, keepdims=True)
        values = values * lax.rsqrt(var + 1e-05) * gain + shift
        for lane in range(0, chans, LANES):
            normed[lane // LANES, first * res : (first + step) * res, :] = values[
                :, lane : lane + LANES
            ]

    weight_t = jnp.concatenate([wl_ref[...], wr_ref[...]], axis=1).astype(F32).T.astype(BF16)
    bias_t = jnp.concatenate([bl_ref[...], br_ref[...]], axis=1)
    bias_t = jnp.broadcast_to(bias_t, (8, 2 * ch)).T[:, 0:1]
    mask_t = mask_ref[...].astype(F32).T
    for r in range(res):
        picked = jnp.concatenate(
            [normed[h, pl.ds(r, seqs, stride=res), :] for h in range(chans // LANES)], axis=1
        ).astype(BF16)
        proj = (dot_nt(weight_t, picked) + bias_t) * mask_t[r : r + 1, :]
        left_buf[col, r * ch : (r + 1) * ch, :] = proj[:ch].astype(BF16)
        shuffle[pl.ds(r, ch, stride=res), :] = proj[ch:]
    mask_rows = jnp.concatenate([mask_t, jnp.zeros_like(mask_t)], axis=0)[:ROW_TILE].astype(BF16)
    left_buf[col, block : block + ROW_TILE, :] = mask_rows
    own_right[0:block, :] = shuffle[...].astype(BF16)
    own_right[block : block + ROW_TILE, :] = mask_rows

    pl.semaphore_wait(barrier, n_row * n_col - 1 + n_seq - 1)

    def left_copy(k):
        return pltpu.make_async_remote_copy(
            src_ref=left_buf.at[col], dst_ref=left_buf.at[col], send_sem=send_left.at[k],
            recv_sem=recv_left.at[col], device_id={"col": (col + k) % n_col}, device_id_type=MESH,
        )

    def left_arrival(k):
        other = (col + k) % n_col
        return pltpu.make_async_remote_copy(
            src_ref=left_buf.at[other], dst_ref=left_buf.at[other], send_sem=send_left.at[k],
            recv_sem=recv_left.at[other], device_id={"col": other}, device_id_type=MESH,
        )

    def right_copy(k):
        return pltpu.make_async_remote_copy(
            src_ref=own_right, dst_ref=right_buf.at[my_slot], send_sem=send_right.at[k],
            recv_sem=recv_right.at[my_slot],
            device_id={"row": (row + k) % n_row, "col": dest_col}, device_id_type=MESH,
        )

    def right_wait(slot):
        pltpu.make_async_copy(own_right, right_buf.at[slot], recv_right.at[slot]).wait()

    for k in range(1, n_row):
        right_copy(k).start()

    @pl.when(dest_col != col)
    def _():
        right_copy(0).start()

    @pl.when(dest_col == col)
    def _():
        pltpu.make_async_copy(own_right, right_buf.at[my_slot], recv_right.at[my_slot]).start()

    for k in range(1, n_col):
        left_copy(k).start()

    wide[...] = wout_ref[...].astype(F32)
    big_w[...] = jnp.zeros_like(big_w)
    for e in range(ch):
        piece = wide[pl.ds(e, ch, stride=ch), :].astype(BF16)
        for g in range(groups):
            start = e * LANES + g * ch
            big_w[start : start + ch, g * pair_ch : (g + 1) * pair_ch] = piece

    for k in range(1, n_col):
        left_arrival(k).wait_recv()
    left = jnp.concatenate([left_buf[n, 0:block, :] for n in range(n_col)], axis=0)
    left_mask = jnp.concatenate(
        [left_buf[n, block : block + ROW_TILE, :].astype(F32)[:res] for n in range(n_col)], axis=0
    )
    left_mask = jnp.concatenate(
        [left_mask, jnp.zeros((LANES - rows_i, seqs), F32)], axis=0
    ).astype(BF16)

    def chunk_update(chunk):
        outers, masks = [], []
        for n in range(n_col):
            slot = chunk * n_col + n
            right_wait(slot)
            outers.append(dot_nt(right_buf[slot, 0:block, :], left))
            masks.append(right_buf[slot, block : block + ROW_TILE, :].astype(F32)[:res])
        half_rows = ig_count * chip_res
        for e in range(ch):
            both = jnp.concatenate([o[e * res : (e + 1) * res, :] for o in outers], axis=0)
            high = both.astype(BF16)
            low = (both - high.astype(F32)).astype(BF16)
            for ig in range(ig_count):
                rows = slice(ig * chip_res, (ig + 1) * chip_res)
                low_rows = slice(half_rows + ig * chip_res, half_rows + (ig + 1) * chip_res)
                lanes = slice(e * LANES, (e + 1) * LANES)
                spread[rows, lanes] = high[:, ig * LANES : (ig + 1) * LANES]
                spread[low_rows, lanes] = low[:, ig * LANES : (ig + 1) * LANES]
        product = jnp.dot(spread[...], big_w[...], preferred_element_type=F32)
        product = product[:half_rows] + product[half_rows:]
        right_mask = jnp.concatenate(masks, axis=0).astype(BF16)
        return product, dot_nt(right_mask, left_mask)

    def tile(product, i):
        ig, g = i // groups, i % groups
        return product[
            ig * chip_res : (ig + 1) * chip_res, g * pair_ch : (g + 1) * pair_ch
        ]

    def part_copy(k):
        return pltpu.make_async_remote_copy(
            src_ref=part.at[k], dst_ref=part_in.at[k], send_sem=send_part.at[k],
            recv_sem=recv_part.at[k], device_id={"seq": (seq + k) % n_seq}, device_id_type=MESH,
        )

    def count_copy(k):
        return pltpu.make_async_remote_copy(
            src_ref=count.at[k], dst_ref=count_in.at[k], send_sem=send_count.at[k],
            recv_sem=recv_count.at[k], device_id={"seq": (seq + k) % n_seq}, device_id_type=MESH,
        )

    for k in range(1, n_seq):
        for piece in range(chunks):
            product, counts = chunk_update(((seq + k) % n_seq) * chunks + piece)
            place = slice(piece * chip_res, (piece + 1) * chip_res)
            for i in range(rows_i):
                part[k, i, place, :] = tile(product, i).astype(BF16)
            count[k, place, :] = counts
        part_copy(k).start()
        count_copy(k).start()

    for piece in range(chunks):
        product, counts = chunk_update(seq * chunks + piece)
        place = slice(piece * chip_res, (piece + 1) * chip_res)
        if piece == 0:
            for k in range(1, n_seq):
                part_copy(k).wait_recv()
                count_copy(k).wait_recv()
        for k in range(1, n_seq):
            counts = counts + count_in[k, place, :]
        scale = 1.0 / (counts + 0.001)
        for i in range(rows_i):
            total = tile(product, i)
            for k in range(1, n_seq):
                total = total + part_in[k, i, place, :].astype(F32)
            out_ref[i, place, :] = (
                pair_ref[i, place, :].astype(F32) + total * scale[:, i : i + 1]
            ).astype(BF16)

    for k in range(1, n_row):
        right_copy(k).wait_send()

    @pl.when(dest_col != col)
    def _():
        right_copy(0).wait_send()

    for k in range(1, n_col):
        left_copy(k).wait_send()
    for k in range(1, n_seq):
        part_copy(k).wait_send()
        count_copy(k).wait_send()


def on_device(
    sizes,
    alignment, alignment_mask, norm_gain, norm_bias, left_weight, left_bias, right_weight,
    right_bias, out_weight, pair_state,
):
    n_row, n_col, n_seq = sizes
    seqs, res, chans = alignment.shape
    ch = left_weight.shape[1]
    rows_i, cols_j, pair_ch = pair_state.shape
    block = res * ch + ROW_TILE
    groups = LANES // ch
    dma = pltpu.SemaphoreType.DMA
    vmem = pl.BlockSpec(memory_space=pltpu.VMEM)
    return pl.pallas_call(
        functools.partial(kernel, sizes),
        out_shape=jax.ShapeDtypeStruct(pair_state.shape, BF16),
        in_specs=[vmem] * 10,
        out_specs=vmem,
        scratch_shapes=[
            pltpu.VMEM((chans // LANES, seqs * res, LANES), F32),
            pltpu.VMEM((res * ch, seqs), F32),
            pltpu.VMEM(out_weight.shape, F32),
            pltpu.VMEM((block, seqs), BF16),
            pltpu.VMEM((n_col, block, seqs), BF16),
            pltpu.VMEM((n_row, block, seqs), BF16),
            pltpu.VMEM((2 * (rows_i // groups) * res * n_col, ch * LANES), BF16),
            pltpu.VMEM((ch * LANES, groups * pair_ch), BF16),
            pltpu.VMEM((n_seq, rows_i, cols_j, pair_ch), BF16),
            pltpu.VMEM((n_seq, rows_i, cols_j, pair_ch), BF16),
            pltpu.VMEM((n_seq, cols_j, LANES), F32),
            pltpu.VMEM((n_seq, cols_j, LANES), F32),
            dma((n_col,)), dma((n_col,)), dma((n_row,)), dma((n_row,)),
            dma((n_seq,)), dma((n_seq,)), dma((n_seq,)), dma((n_seq,)),
        ],
        compiler_params=pltpu.CompilerParams(
            collective_id=0, has_side_effects=True, vmem_limit_bytes=40 * 1024 * 1024
        ),
    )(
        alignment, alignment_mask, norm_gain.reshape(1, chans), norm_bias.reshape(1, chans),
        left_weight, left_bias.reshape(1, ch), right_weight, right_bias.reshape(1, ch),
        out_weight, pair_state,
    )


def solution(mesh):
    sizes = tuple(mesh.shape[name] for name in ("row", "col", "seq"))
    in_specs = (
        P(("groups", "seq"), ("row", "col"), None),
        P(("groups", "seq"), ("row", "col")),
        P(), P(), P(), P(), P(), P(), P(),
        P(("groups", "row"), ("col", "seq"), None),
    )
    return jax.shard_map(
        functools.partial(on_device, sizes),
        mesh=mesh,
        in_specs=in_specs,
        out_specs=P(("groups", "row"), ("col", "seq"), None),
        check_vma=False,
    )
```

time: 78.3 us -> 20.8 us (0.27)
  blocking collectives: 33 us -> 0 us
  Pallas kernels: 0 us -> 15 us
  between operations: 13.5 us -> 0.02 us
  waiting for transfers between devices: 10.4 us -> 0 us
  matrix products: 9.36 us -> 0 us
  other arithmetic: 5.16 us -> 0 us
    all_gather x4 -> x0, blocking collectives: 33 us -> none  [the longest x1 14.8 us: on_device(): lax.all_gather(right_local, ('row', 'col'), axis=1, tiled=True)]
    pallas_call x0 -> x1, Pallas kernels: none -> 15 us  [on_device(): pl.pallas_call(functools.partial(kernel, sizes), out_shape=jax.ShapeDtype...]
    reduce_scatter x1 -> x0, waiting for transfers between devices: 10.4 us -> none  [on_device(): lax.psum_scatter(numer_part, 'seq', scatter_dimension=1, tiled=True)]
    dot_general x11 -> x0, matrix products: 9.36 us -> none  [the longest x4 5.09 us: block_step(): jnp.dot(outer, weight_flat, precision=lax.Precision.HIGHEST, preferred_el...]
    unnamed x18 -> x24, local copies, waits for them, and re-layouts: 1.49 us -> 5.44 us
    another operation x4 -> x0, local copies, waits for them, and re-layouts: 3.8 us -> none
    reduce_sum x2 -> x0, other arithmetic: 2.66 us -> none  [the longest x1 1.4 us: normalize(): spread = jnp.mean(jnp.square(values - center), axis=-1, keepdims=True)]
    convert_element_type x4 -> x0, other arithmetic: 2.47 us -> none  [the longest x1 1.64 us: on_device(): (pair_state.astype(jnp.float32) + numerator / (counts[:, :, None] + 0.001...]
  transfers between devices with their start and end apart: 2 -> 0, of which waited for: 1 -> 0; matrix products, arithmetic and copies ran while one was open for 23% -> 0% of each run, Pallas kernels for 0% -> 0%
where the time goes in v1:
time: 20.8 us; the launch traced here: 20.4 us
  Pallas kernels  15 us (72%)
  local copies, waits for them, and re-layouts  5.44 us (26%)
    pallas_call x1, Pallas kernels, on_device(): pl.pallas_call(functools.partial(kernel, sizes), out_shape=jax.ShapeDtype...  15 us
    unnamed x24, local copies, waits for them, and re-layouts  5.44 us

profile of v1, /device:TPU:1, one launch (start us, length us, event | category | flops | bytes accessed | tf_op | source)
XLA Modules:
  0.0 20.4 jit_solution(10984730283500589846)
XLA Ops:
  0.0 0.0 copy-start.9
  0.0 0.7 %copy-done.9 = bf16[128,8]{0,1:T(8,128)(2,1)S(1)} copy-done((bf16[128,8]{0,1:T(8,128)(2,1)S(1)}, bf16[128,8]{0,1:T(8,128)(2,1)}, u32[]{:S(2)}) %copy-start.9) | copy-done | bytes 2072
  0.7 0.0 copy-start.7
  0.7 0.1 copy.11.mask_ref
  0.8 0.6 %copy-done.7 = bf16[256,32]{0,1:T(8,128)(2,1)S(1)} copy-done((bf16[256,32]{0,1:T(8,128)(2,1)S(1)}, bf16[256,32]{0,1:T(8,128)(2,1)}, u32[]{:S(2)}) %copy-start.7) | copy-done | bytes 16408
  1.4 0.0 copy-start.8
  1.4 0.0 copy-start.2
  1.4 0.1 copy.12.wl_ref
  1.5 0.6 %copy-done.8 = bf16[256,32]{0,1:T(8,128)(2,1)S(1)} copy-done((bf16[256,32]{0,1:T(8,128)(2,1)S(1)}, bf16[256,32]{0,1:T(8,128)(2,1)}, u32[]{:S(2)}) %copy-start.8) | copy-done | bytes 16408
  2.1 0.0 copy-start.3
  2.1 0.0 copy-start.4
  2.1 0.0 copy-start.5
  2.1 0.0 copy-start.6
  2.1 0.1 copy.13.wr_ref
  2.2 0.0 copy-done.2
  2.3 0.5 %copy-done.3 = f32[256]{0:T(256)S(1)} copy-done((f32[256]{0:T(256)S(1)}, f32[256]{0:T(256)}, u32[]{:S(2)}) %copy-start.3) | copy-done | bytes 1048
  2.8 0.0 copy-done.4
  2.8 0.0 copy-done.5
  2.8 0.0 copy-done.6
  2.8 0.0 copy-start
  2.8 1.0 %copy-done = bf16[128,8,256]{2,1,0:T(8,128)(2,1)S(1)} copy-done((bf16[128,8,256]{2,1,0:T(8,128)(2,1)S(1)}, bf16[128,8,256]{2,1,0:T(8,128)(2,1)}, u32[]{:S(2)}) %copy-start) | copy-done | bytes 524312
  3.9 0.0 copy-start.1
  3.9 0.9 %copy-done.1 = bf16[1024,128]{1,0:T(8,128)(2,1)S(1)} copy-done((bf16[1024,128]{1,0:T(8,128)(2,1)S(1)}, bf16[1024,128]{1,0:T(8,128)(2,1)}, u32[]{:S(2)}) %copy-start.1) | copy-done | bytes 262168
  4.8 15.0 %shard_map.100 = bf16[16,16,128]{2,1,0:T(8,128)(2,1)S(1)} custom-call(bf16[128,8,256]{2,1,0:T(8,128)(2,1)S(1)} %copy-done, bf16[128,8]{1,0:T(8,128)(2,1)S(1)} %copy.11.mask_ref, f32[1,256]{1,0:T(1,128)S(1)} %bitcast.4, f32[1,256]{1,0:T(1,128)S(1)} %bitcast.5, bf16[256,32]{1,0:T(8,128)(2,1)S(1)} %copy.12.wl_ref, f32[1,32]{1,0:T(1,128)S(1)} %bitcast.6, ...), custom_call_target="tpu_custom_call" | custom-call | tf_op jit(solution)/shard_map/pallas_call | solution.py:237
  19.8 0.6 %copy.15 = bf16[16,16,128]{2,1,0:T(8,128)(2,1)} copy(bf16[16,16,128]{2,1,0:T(8,128)(2,1)S(1)} %shard_map.100) | data formatting | bytes 131072
Async XLA Ops:
  0.0 0.7 %copy-start.9 = (bf16[128,8]{0,1:T(8,128)(2,1)S(1)}, bf16[128,8]{0,1:T(8,128)(2,1)}, u32[]{:S(2)}) copy-start(bf16[128,8]{0,1:T(8,128)(2,1)} %param.11) | copy-start | bytes 6148
  0.7 0.7 %copy-start.7 = (bf16[256,32]{0,1:T(8,128)(2,1)S(1)}, bf16[256,32]{0,1:T(8,128)(2,1)}, u32[]{:S(2)}) copy-start(bf16[256,32]{0,1:T(8,128)(2,1)} %param.14) | copy-start | bytes 49156
  1.4 0.7 %copy-start.8 = (bf16[256,32]{0,1:T(8,128)(2,1)S(1)}, bf16[256,32]{0,1:T(8,128)(2,1)}, u32[]{:S(2)}) copy-start(bf16[256,32]{0,1:T(8,128)(2,1)} %param.16) | copy-start | bytes 49156
  1.4 0.9 %copy-start.2 = (bf16[16,16,128]{2,1,0:T(8,128)(2,1)S(1)}, bf16[16,16,128]{2,1,0:T(8,128)(2,1)}, u32[]{:S(2)}) copy-start(bf16[16,16,128]{2,1,0:T(8,128)(2,1)} %pair_ref.1) | copy-start | bytes 196612
  2.1 0.7 %copy-start.3 = (f32[256]{0:T(256)S(1)}, f32[256]{0:T(256)}, u32[]{:S(2)}) copy-start(f32[256]{0:T(256)} %param.12) | copy-start | bytes 3076
  2.1 0.7 %copy-start.4 = (f32[256]{0:T(256)S(1)}, f32[256]{0:T(256)}, u32[]{:S(2)}) copy-start(f32[256]{0:T(256)} %param.13) | copy-start | bytes 3076
  2.1 0.7 %copy-start.5 = (f32[32]{0:T(128)S(1)}, f32[32]{0:T(128)}, u32[]{:S(2)}) copy-start(f32[32]{0:T(128)} %param.15) | copy-start | bytes 388
  2.1 0.7 %copy-start.6 = (f32[32]{0:T(128)S(1)}, f32[32]{0:T(128)}, u32[]{:S(2)}) copy-start(f32[32]{0:T(128)} %param.17) | copy-start | bytes 388
  2.8 1.0 %copy-start = (bf16[128,8,256]{2,1,0:T(8,128)(2,1)S(1)}, bf16[128,8,256]{2,1,0:T(8,128)(2,1)}, u32[]{:S(2)}) copy-start(bf16[128,8,256]{2,1,0:T(8,128)(2,1)} %x_ref.1) | copy-start | bytes 1572868
  3.9 0.9 %copy-start.1 = (bf16[1024,128]{1,0:T(8,128)(2,1)S(1)}, bf16[1024,128]{1,0:T(8,128)(2,1)}, u32[]{:S(2)}) copy-start(bf16[1024,128]{1,0:T(8,128)(2,1)} %wout_ref.1) | copy-start | bytes 786436

commit v2 on v1

v2 whole, which is shorter than its diff:
```python
import functools

import jax
import jax.numpy as jnp
from jax import lax
from jax.experimental import pallas as pl
from jax.experimental.pallas import tpu as pltpu
from jax.sharding import PartitionSpec as P

MESH = pl.DeviceIdType.MESH
F32 = jnp.float32
BF16 = jnp.bfloat16
ROW_TILE = 16
LANES = 128
X_PARTS = 4


def dot_nt(a, b):
    return lax.dot_general(a, b, (((1,), (1,)), ((), ())), preferred_element_type=F32)


def kernel(
    sizes,
    x_hbm, mask_hbm, gain_hbm, bias_hbm, wl_hbm, bl_hbm, wr_hbm, br_hbm, wout_hbm, pair_hbm,
    out_ref,
    x_ref, mask_ref, gain_ref, bias_ref, weight_ref, bl_ref, br_ref, wout_ref, pair_ref,
    normed, shuffle, wide, own_right, left_buf, right_buf, spread, big_w,
    in_sem, send_left, recv_left, send_right, recv_right,
):
    n_row, n_col, n_seq = sizes
    seqs, res, chans = x_ref.shape
    ch = wl_hbm.shape[0]
    rows_i, cols_j, pair_ch = pair_ref.shape
    block = res * ch
    chip_res = res * n_col
    chunks = cols_j // chip_res
    cores = n_col * n_seq
    groups = LANES // ch
    ig_count = rows_i // groups
    row, col, seq = lax.axis_index("row"), lax.axis_index("col"), lax.axis_index("seq")
    here = col * n_seq + seq
    dest_col, dest_seq = row // chunks // n_seq, row // chunks % n_seq
    stays = dest_col * n_seq + dest_seq == here
    my_chunk = row % chunks

    copies = [
        pltpu.make_async_copy(mask_hbm, mask_ref, in_sem.at[0]),
        pltpu.make_async_copy(gain_hbm, gain_ref, in_sem.at[1]),
        pltpu.make_async_copy(bias_hbm, bias_ref, in_sem.at[2]),
        pltpu.make_async_copy(wl_hbm, weight_ref.at[0:ch], in_sem.at[3]),
        pltpu.make_async_copy(wr_hbm, weight_ref.at[ch : 2 * ch], in_sem.at[4]),
        pltpu.make_async_copy(bl_hbm, bl_ref, in_sem.at[5]),
        pltpu.make_async_copy(br_hbm, br_ref, in_sem.at[6]),
    ]
    late = [
        pltpu.make_async_copy(wout_hbm, wout_ref, in_sem.at[7]),
        pltpu.make_async_copy(pair_hbm, pair_ref, in_sem.at[8]),
    ]
    part = seqs // X_PARTS
    x_copies = [
        pltpu.make_async_copy(
            x_hbm.at[n * part : (n + 1) * part], x_ref.at[n * part : (n + 1) * part],
            in_sem.at[9 + n],
        )
        for n in range(X_PARTS)
    ]
    for copy in x_copies[:1] + copies + x_copies[1:] + late:
        copy.start()

    barrier = pltpu.get_barrier_semaphore()
    for piece in range(chunks):
        source = here * chunks + piece
        for n in range(cores):
            @pl.when((source != row) | (here != n))
            def _():
                pl.semaphore_signal(
                    barrier, inc=1, device_id_type=MESH,
                    device_id={"row": source, "col": n // n_seq, "seq": n % n_seq},
                )
    for k in range(1, cores):
        other = (here + k) % cores
        pl.semaphore_signal(
            barrier, inc=1, device_id={"col": other // n_seq, "seq": other % n_seq},
            device_id_type=MESH,
        )

    for copy in copies:
        copy.wait()
    gain, shift = gain_ref[...], bias_ref[...]
    step = 16
    for first in range(0, seqs, step):
        if first % part == 0:
            x_copies[first // part].wait()
        values = x_ref[first : first + step].astype(F32).reshape(step * res, chans)
        center = jnp.mean(values, axis=-1, keepdims=True)
        values = values - center
        var = jnp.mean(values * values, axis=-1, keepdims=True)
        values = values * lax.rsqrt(var + 1e-05) * gain + shift
        for lane in range(0, chans, LANES):
            normed[lane // LANES, first * res : (first + step) * res, :] = values[
                :, lane : lane + LANES
            ]

    weight_t = weight_ref[...]
    bias_t = jnp.concatenate([bl_ref[...], br_ref[...]], axis=1)
    bias_t = jnp.broadcast_to(bias_t, (8, 2 * ch)).T[:, 0:1]
    mask_t = mask_ref[...].astype(F32)
    for r in range(res):
        picked = jnp.concatenate(
            [normed[h, pl.ds(r, seqs, stride=res), :] for h in range(chans // LANES)], axis=1
        ).astype(BF16)
        proj = (dot_nt(weight_t, picked) + bias_t) * mask_t[r : r + 1, :]
        left_buf[col, seq, r * ch : (r + 1) * ch, :] = proj[:ch].astype(BF16)
        shuffle[pl.ds(r, ch, stride=res), :] = proj[ch:]
    mask_rows = jnp.concatenate([mask_t, jnp.zeros_like(mask_t)], axis=0)[:ROW_TILE].astype(BF16)
    left_buf[col, seq, block : block + ROW_TILE, :] = mask_rows
    own_right[0:block, :] = shuffle[...].astype(BF16)
    own_right[block : block + ROW_TILE, :] = mask_rows

    def left_copy(k):
        other = (here + k) % cores
        return pltpu.make_async_remote_copy(
            src_ref=left_buf.at[col, seq], dst_ref=left_buf.at[col, seq],
            send_sem=send_left.at[k], recv_sem=recv_left.at[col, seq],
            device_id={"col": other // n_seq, "seq": other % n_seq}, device_id_type=MESH,
        )

    def right_copy(k):
        return pltpu.make_async_remote_copy(
            src_ref=own_right, dst_ref=right_buf.at[my_chunk, col, seq],
            send_sem=send_right.at[k], recv_sem=recv_right.at[my_chunk, col, seq],
            device_id={"row": (row + k) % n_row, "col": dest_col, "seq": dest_seq},
            device_id_type=MESH,
        )

    def right_local():
        return pltpu.make_async_copy(
            own_right, right_buf.at[my_chunk, col, seq], recv_right.at[my_chunk, col, seq]
        )

    @pl.when(stays)
    def _():
        right_local().start()
        pl.semaphore_wait(barrier, n_row - 1 + cores - 1)

    @pl.when(jnp.logical_not(stays))
    def _():
        pl.semaphore_wait(barrier, n_row + cores - 1)
        right_copy(0).start()

    for k in range(1, n_row):
        right_copy(k).start()
    for k in range(1, cores):
        left_copy(k).start()

    for copy in late:
        copy.wait()
    wide[...] = wout_ref[...].astype(F32)
    big_w[...] = jnp.zeros_like(big_w)
    for e in range(ch):
        piece = wide[pl.ds(e, ch, stride=ch), :].astype(BF16)
        for g in range(groups):
            start = e * LANES + g * ch
            big_w[start : start + ch, g * pair_ch : (g + 1) * pair_ch] = piece

    for k in range(1, cores):
        other = (here + k) % cores
        slot = (other // n_seq, other % n_seq)
        pltpu.make_async_copy(own_right, left_buf.at[slot], recv_left.at[slot]).wait()

    def both_seqs(buf, at, rows):
        return jnp.concatenate([buf[(*at, q, rows)] for q in range(n_seq)], axis=1)

    def masks(buf, at, rows_to):
        found = [
            both_seqs(buf, (*at, n), slice(block, block + ROW_TILE)).astype(F32)[:res]
            for n in range(n_col)
        ]
        if rows_to > chip_res:
            found.append(jnp.zeros((rows_to - chip_res, n_seq * seqs), F32))
        return jnp.concatenate(found, axis=0).astype(BF16)

    left = jnp.concatenate(
        [both_seqs(left_buf, (n,), slice(0, block)) for n in range(n_col)], axis=0
    )
    left_mask = masks(left_buf, (), LANES)
    half_rows = ig_count * chip_res

    for piece in range(chunks):
        outers = []
        for n in range(n_col):
            for q in range(n_seq):
                pltpu.make_async_copy(
                    own_right, right_buf.at[piece, n, q], recv_right.at[piece, n, q]
                ).wait()
            outers.append(dot_nt(both_seqs(right_buf, (piece, n), slice(0, block)), left))
        for e in range(ch):
            both = jnp.concatenate([o[e * res : (e + 1) * res, :] for o in outers], axis=0)
            high = both.astype(BF16)
            low = (both - high.astype(F32)).astype(BF16)
            for ig in range(ig_count):
                rows = slice(ig * chip_res, (ig + 1) * chip_res)
                low_rows = slice(half_rows + ig * chip_res, half_rows + (ig + 1) * chip_res)
                lanes = slice(e * LANES, (e + 1) * LANES)
                spread[rows, lanes] = high[:, ig * LANES : (ig + 1) * LANES]
                spread[low_rows, lanes] = low[:, ig * LANES : (ig + 1) * LANES]
        product = jnp.dot(spread[...], big_w[...], preferred_element_type=F32)
        product = product[:half_rows] + product[half_rows:]
        counts = dot_nt(masks(right_buf, (piece,), chip_res), left_mask)
        scale = 1.0 / (counts + 0.001)
        place = slice(piece * chip_res, (piece + 1) * chip_res)
        for i in range(rows_i):
            ig, g = i // groups, i % groups
            update = product[
                ig * chip_res : (ig + 1) * chip_res, g * pair_ch : (g + 1) * pair_ch
            ]
            out_ref[i, place, :] = (
                pair_ref[i, place, :].astype(F32) + update * scale[:, i : i + 1]
            ).astype(BF16)

    for k in range(1, n_row):
        right_copy(k).wait_send()

    @pl.when(jnp.logical_not(stays))
    def _():
        right_copy(0).wait_send()

    for k in range(1, cores):
        left_copy(k).wait_send()


def on_device(
    sizes,
    alignment, alignment_mask, norm_gain, norm_bias, left_weight, left_bias, right_weight,
    right_bias, out_weight, pair_state,
):
    n_row, n_col, n_seq = sizes
    seqs, res, chans = alignment.shape
    ch = left_weight.shape[1]
    rows_i, cols_j, pair_ch = pair_state.shape
    block = res * ch + ROW_TILE
    chunks = cols_j // (res * n_col)
    groups = LANES // ch
    dma = pltpu.SemaphoreType.DMA
    return pl.pallas_call(
        functools.partial(kernel, sizes),
        out_shape=jax.ShapeDtypeStruct(pair_state.shape, BF16),
        in_specs=[pl.BlockSpec(memory_space=pl.ANY)] * 10,
        out_specs=pl.BlockSpec(memory_space=pltpu.VMEM),
        scratch_shapes=[
            pltpu.VMEM(alignment.shape, BF16),
            pltpu.VMEM((res, seqs), BF16),
            pltpu.VMEM((1, chans), F32),
            pltpu.VMEM((1, chans), F32),
            pltpu.VMEM((2 * ch, chans), BF16),
            pltpu.VMEM((1, ch), F32),
            pltpu.VMEM((1, ch), F32),
            pltpu.VMEM(out_weight.shape, BF16),
            pltpu.VMEM(pair_state.shape, BF16),
            pltpu.VMEM((chans // LANES, seqs * res, LANES), F32),
            pltpu.VMEM((res * ch, seqs), F32),
            pltpu.VMEM(out_weight.shape, F32),
            pltpu.VMEM((block, seqs), BF16),
            pltpu.VMEM((n_col, n_seq, block, seqs), BF16),
            pltpu.VMEM((chunks, n_col, n_seq, block, seqs), BF16),
            pltpu.VMEM((2 * (rows_i // groups) * res * n_col, ch * LANES), BF16),
            pltpu.VMEM((ch * LANES, groups * pair_ch), BF16),
            dma((9 + X_PARTS,)), dma((n_col * n_seq,)), dma((n_col, n_seq)), dma((n_row,)),
            dma((chunks, n_col, n_seq)),
        ],
        compiler_params=pltpu.CompilerParams(
            collective_id=0, has_side_effects=True, vmem_limit_bytes=56 * 1024 * 1024
        ),
    )(
        alignment, alignment_mask.T, norm_gain.reshape(1, chans), norm_bias.reshape(1, chans),
        left_weight.T, left_bias.reshape(1, ch), right_weight.T, right_bias.reshape(1, ch),
        out_weight, pair_state,
    )


def solution(mesh):
    sizes = tuple(mesh.shape[name] for name in ("row", "col", "seq"))
    in_specs = (
        P(("groups", "seq"), ("row", "col"), None),
        P(("groups", "seq"), ("row", "col")),
        P(), P(), P(), P(), P(), P(), P(),
        P(("groups", "row"), ("col", "seq"), None),
    )
    return jax.shard_map(
        functools.partial(on_device, sizes),
        mesh=mesh,
        in_specs=in_specs,
        out_specs=P(("groups", "row"), ("col", "seq"), None),
        check_vma=False,
    )
```

time: 20.8 us -> 17.3 us (0.83)
  the two profiles are of different devices: /device:TPU:1 before, /device:TPU:0 now
where the time goes in v2:
time: 17.3 us; the launch traced here: 17.2 us
  Pallas kernels  15.7 us (91%)
  local copies, waits for them, and re-layouts  1.47 us (8%)
    pallas_call x1, Pallas kernels, on_device(): pl.pallas_call(functools.partial(kernel, sizes), out_shape=jax.ShapeDtype...  15.7 us
    unnamed x1, local copies, waits for them, and re-layouts  1.47 us

profile of v2, /device:TPU:0, one launch (start us, length us, event | category | flops | bytes accessed | tf_op | source)
XLA Modules:
  0.0 17.2 jit_solution(17648873697018779175)
XLA Ops:
  0.0 15.7 %shard_map.100 = bf16[16,16,128]{2,1,0:T(8,128)(2,1)} custom-call(bf16[128,8,256]{2,1,0:T(8,128)(2,1)} %x_hbm.1, bf16[8,128]{1,0:T(8,128)(2,1)} %bitcast.9, f32[1,256]{1,0:T(1,128)} %bitcast.10, f32[1,256]{1,0:T(1,128)} %bitcast.11, bf16[32,256]{1,0:T(8,128)(2,1)} %bitcast.7, f32[1,32]{1,0:T(1,128)} %bitcast.12, bf16[32,256]{1,0:T(8,128)(2,1)} %bitcast.8, ...), custom_call_target="tpu_custom_call" | custom-call | tf_op jit(solution)/shard_map/pallas_call | solution.py:245
  15.7 1.5 %copy.12 = bf16[16,16,128]{2,1,0:T(8,128)(2,1)} copy(bf16[16,16,128]{2,1,0:T(8,128)(2,1)} %shard_map.100) | data formatting | bytes 131072

commit v3 on v2

--- a/solution.py
+++ b/solution.py
@@ -25,7 +25,7 @@
     out_ref,
     x_ref, mask_ref, gain_ref, bias_ref, weight_ref, bl_ref, br_ref, wout_ref, pair_ref,
     normed, shuffle, wide, own_right, left_buf, right_buf, spread, big_w,
-    in_sem, send_left, recv_left, send_right, recv_right,
+    in_sem, send_left, recv_left, send_right, recv_right, send_seq,
 ):
     n_row, n_col, n_seq = sizes
     seqs, res, chans = x_ref.shape
@@ -77,11 +77,14 @@
                     barrier, inc=1, device_id_type=MESH,
                     device_id={"row": source, "col": n // n_seq, "seq": n % n_seq},
                 )
-    for k in range(1, cores):
-        other = (here + k) % cores
+    near = n_col - 1 + n_seq - 1
+    for n in range(1, n_col):
         pl.semaphore_signal(
-            barrier, inc=1, device_id={"col": other // n_seq, "seq": other % n_seq},
-            device_id_type=MESH,
+            barrier, inc=1, device_id={"col": (col + n) % n_col}, device_id_type=MESH
+        )
+    for k in range(1, n_seq):
+        pl.semaphore_signal(
+            barrier, inc=1, device_id={"seq": (seq + k) % n_seq}, device_id_type=MESH
         )
 
     for copy in copies:
@@ -117,13 +120,22 @@
     own_right[0:block, :] = shuffle[...].astype(BF16)
     own_right[block : block + ROW_TILE, :] = mask_rows
 
-    def left_copy(k):
-        other = (here + k) % cores
+    def to_seq(k):
         return pltpu.make_async_remote_copy(
             src_ref=left_buf.at[col, seq], dst_ref=left_buf.at[col, seq],
-            send_sem=send_left.at[k], recv_sem=recv_left.at[col, seq],
-            device_id={"col": other // n_seq, "seq": other % n_seq}, device_id_type=MESH,
-        )
+            send_sem=send_seq.at[k], recv_sem=recv_left.at[col, seq],
+            device_id={"seq": (seq + k) % n_seq}, device_id_type=MESH,
+        )
+
+    def to_core(n, q):
+        return pltpu.make_async_remote_copy(
+            src_ref=left_buf.at[col, q], dst_ref=left_buf.at[col, q],
+            send_sem=send_left.at[n, q], recv_sem=recv_left.at[col, q],
+            device_id={"col": (col + n) % n_col}, device_id_type=MESH,
+        )
+
+    def left_wait(n, q):
+        pltpu.make_async_copy(own_right, left_buf.at[n, q], recv_left.at[n, q]).wait()
 
     def right_copy(k):
         return pltpu.make_async_remote_copy(
@@ -141,17 +153,19 @@
     @pl.when(stays)
     def _():
         right_local().start()
-        pl.semaphore_wait(barrier, n_row - 1 + cores - 1)
+        pl.semaphore_wait(barrier, n_row - 1 + near)
 
     @pl.when(jnp.logical_not(stays))
     def _():
-        pl.semaphore_wait(barrier, n_row + cores - 1)
+        pl.semaphore_wait(barrier, n_row + near)
         right_copy(0).start()
 
+    for n in range(1, n_col):
+        to_core(n, seq).start()
+    for k in range(1, n_seq):
+        to_seq(k).start()
     for k in range(1, n_row):
         right_copy(k).start()
-    for k in range(1, cores):
-        left_copy(k).start()
 
     for copy in late:
         copy.wait()
@@ -163,10 +177,14 @@
             start = e * LANES + g * ch
             big_w[start : start + ch, g * pair_ch : (g + 1) * pair_ch] = piece
 
-    for k in range(1, cores):
-        other = (here + k) % cores
-        slot = (other // n_seq, other % n_seq)
-        pltpu.make_async_copy(own_right, left_buf.at[slot], recv_left.at[slot]).wait()
+    for k in range(1, n_seq):
+        other = (seq + k) % n_seq
+        left_wait(col, other)
+        for n in range(1, n_col):
+            to_core(n, other).start()
+    for n in range(1, n_col):
+        for q in range(n_seq):
+            left_wait((col + n) % n_col, q)
 
     def both_seqs(buf, at, rows):
         return jnp.concatenate([buf[(*at, q, rows)] for q in range(n_seq)], axis=1)
@@ -225,8 +243,11 @@
     def _():
         right_copy(0).wait_send()
 
-    for k in range(1, cores):
-        left_copy(k).wait_send()
+    for k in range(1, n_seq):
+        to_seq(k).wait_send()
+    for n in range(1, n_col):
+        for q in range(n_seq):
+            to_core(n, q).wait_send()
 
 
 def on_device(
@@ -265,8 +286,8 @@
             pltpu.VMEM((chunks, n_col, n_seq, block, seqs), BF16),
             pltpu.VMEM((2 * (rows_i // groups) * res * n_col, ch * LANES), BF16),
             pltpu.VMEM((ch * LANES, groups * pair_ch), BF16),
-            dma((9 + X_PARTS,)), dma((n_col * n_seq,)), dma((n_col, n_seq)), dma((n_row,)),
-            dma((chunks, n_col, n_seq)),
+            dma((9 + X_PARTS,)), dma((n_col, n_seq)), dma((n_col, n_seq)), dma((n_row,)),
+            dma((chunks, n_col, n_seq)), dma((n_seq,)),
         ],
         compiler_params=pltpu.CompilerParams(
             collective_id=0, has_side_effects=True, vmem_limit_bytes=56 * 1024 * 1024

time: 17.3 us -> 16.2 us (0.936)
  the two profiles are of different devices: /device:TPU:0 before, /device:TPU:1 now
where the time goes in v3:
time: 16.2 us; the launch traced here: 16 us
  Pallas kernels  14.5 us (90%)
  local copies, waits for them, and re-layouts  1.47 us (9%)
    pallas_call x1, Pallas kernels, on_device(): pl.pallas_call(functools.partial(kernel, sizes), out_shape=jax.ShapeDtype...  14.5 us
    unnamed x1, local copies, waits for them, and re-layouts  1.47 us

profile of v3, /device:TPU:1, one launch (start us, length us, event | category | flops | bytes accessed | tf_op | source)
XLA Modules:
  0.0 16.0 jit_solution(3148851931342680621)
XLA Ops:
  0.0 14.5 %shard_map.100 = bf16[16,16,128]{2,1,0:T(8,128)(2,1)} custom-call(bf16[128,8,256]{2,1,0:T(8,128)(2,1)} %x_hbm.1, bf16[8,128]{1,0:T(8,128)(2,1)} %bitcast.9, f32[1,256]{1,0:T(1,128)} %bitcast.10, f32[1,256]{1,0:T(1,128)} %bitcast.11, bf16[32,256]{1,0:T(8,128)(2,1)} %bitcast.7, f32[1,32]{1,0:T(1,128)} %bitcast.12, bf16[32,256]{1,0:T(8,128)(2,1)} %bitcast.8, ...), custom_call_target="tpu_custom_call" | custom-call | tf_op jit(solution)/shard_map/pallas_call | solution.py:266
  14.5 1.5 %copy.12 = bf16[16,16,128]{2,1,0:T(8,128)(2,1)} copy(bf16[16,16,128]{2,1,0:T(8,128)(2,1)} %shard_map.100) | data formatting | bytes 131072

commit v4 on v3

--- a/solution.py
+++ b/solution.py
@@ -25,7 +25,7 @@
     out_ref,
     x_ref, mask_ref, gain_ref, bias_ref, weight_ref, bl_ref, br_ref, wout_ref, pair_ref,
     normed, shuffle, wide, own_right, left_buf, right_buf, spread, big_w,
-    in_sem, send_left, recv_left, send_right, recv_right, send_seq,
+    in_sem, send_left, recv_left, send_right, recv_right, send_seq, ready,
 ):
     n_row, n_col, n_seq = sizes
     seqs, res, chans = x_ref.shape
@@ -42,6 +42,7 @@
     dest_col, dest_seq = row // chunks // n_seq, row // chunks % n_seq
     stays = dest_col * n_seq + dest_seq == here
     my_chunk = row % chunks
+    in_turn = row == n_row - 1
 
     copies = [
         pltpu.make_async_copy(mask_hbm, mask_ref, in_sem.at[0]),
@@ -64,19 +65,26 @@
         )
         for n in range(X_PARTS)
     ]
-    for copy in x_copies[:1] + copies + x_copies[1:] + late:
+    for copy in x_copies:
         copy.start()
 
     barrier = pltpu.get_barrier_semaphore()
     for piece in range(chunks):
         source = here * chunks + piece
         for n in range(cores):
-            @pl.when((source != row) | (here != n))
+            @pl.when((source > row) | ((source == row) & (here != n)))
             def _():
                 pl.semaphore_signal(
                     barrier, inc=1, device_id_type=MESH,
                     device_id={"row": source, "col": n // n_seq, "seq": n % n_seq},
                 )
+    for to_row in range(1, n_row):
+        @pl.when(to_row > row)
+        def _():
+            pl.semaphore_signal(
+                barrier, inc=1, device_id_type=MESH,
+                device_id={"row": to_row, "col": dest_col, "seq": dest_seq},
+            )
     near = n_col - 1 + n_seq - 1
     for n in range(1, n_col):
         pl.semaphore_signal(
@@ -86,6 +94,20 @@
         pl.semaphore_signal(
             barrier, inc=1, device_id={"seq": (seq + k) % n_seq}, device_id_type=MESH
         )
+
+    for copy in copies + late:
+        copy.start()
+    lower_sources = jnp.clip(row - here * chunks, 0, chunks)
+    pl.semaphore_wait(barrier, near + row + jnp.where(stays, 0, 1) + cores * lower_sources)
+    for piece in range(chunks):
+        source = here * chunks + piece
+        for n in range(cores):
+            @pl.when(source < row)
+            def _():
+                pl.semaphore_signal(
+                    ready.at[row], inc=1, device_id_type=MESH,
+                    device_id={"row": source, "col": n // n_seq, "seq": n % n_seq},
+                )
 
     for copy in copies:
         copy.wait()
@@ -138,10 +160,13 @@
         pltpu.make_async_copy(own_right, left_buf.at[n, q], recv_left.at[n, q]).wait()
 
     def right_copy(k):
+        to_row = row if k == 0 else lax.select(k - 1 < row, k - 1, k)
+        if k > 0:
+            to_row = lax.select(row == n_row - 1, n_row - 1 - k, to_row)
         return pltpu.make_async_remote_copy(
             src_ref=own_right, dst_ref=right_buf.at[my_chunk, col, seq],
             send_sem=send_right.at[k], recv_sem=recv_right.at[my_chunk, col, seq],
-            device_id={"row": (row + k) % n_row, "col": dest_col, "seq": dest_seq},
+            device_id={"row": to_row, "col": dest_col, "seq": dest_seq},
             device_id_type=MESH,
         )
 
@@ -149,22 +174,26 @@
         return pltpu.make_async_copy(
             own_right, right_buf.at[my_chunk, col, seq], recv_right.at[my_chunk, col, seq]
         )
-
-    @pl.when(stays)
-    def _():
-        right_local().start()
-        pl.semaphore_wait(barrier, n_row - 1 + near)
-
-    @pl.when(jnp.logical_not(stays))
-    def _():
-        pl.semaphore_wait(barrier, n_row + near)
-        right_copy(0).start()
 
     for n in range(1, n_col):
         to_core(n, seq).start()
     for k in range(1, n_seq):
         to_seq(k).start()
+    @pl.when(stays)
+    def _():
+        right_local().start()
+
+    @pl.when(jnp.logical_not(stays))
+    def _():
+        right_copy(0).start()
+
     for k in range(1, n_row):
+        @pl.when(k > row)
+        def _():
+            pl.semaphore_wait(ready.at[k], 1)
+
+        if k == 2:
+            pl.when(in_turn)(right_copy(1).wait_send)
         right_copy(k).start()
 
     for copy in late:
@@ -236,7 +265,8 @@
                 pair_ref[i, place, :].astype(F32) + update * scale[:, i : i + 1]
             ).astype(BF16)
 
-    for k in range(1, n_row):
+    pl.when(jnp.logical_not(in_turn))(right_copy(1).wait_send)
+    for k in range(2, n_row):
         right_copy(k).wait_send()
 
     @pl.when(jnp.logical_not(stays))
@@ -288,6 +318,7 @@
             pltpu.VMEM((ch * LANES, groups * pair_ch), BF16),
             dma((9 + X_PARTS,)), dma((n_col, n_seq)), dma((n_col, n_seq)), dma((n_row,)),
             dma((chunks, n_col, n_seq)), dma((n_seq,)),
+            pltpu.SemaphoreType.REGULAR((n_row,)),
         ],
         compiler_params=pltpu.CompilerParams(
             collective_id=0, has_side_effects=True, vmem_limit_bytes=56 * 1024 * 1024

time: 16.2 us -> 15.6 us (0.963)
  the two profiles are of different devices: /device:TPU:1 before, /device:TPU:3 now
where the time goes in v4:
time: 15.6 us; the launch traced here: 15.4 us
  Pallas kernels  14 us (90%)
  local copies, waits for them, and re-layouts  1.47 us (9%)
    pallas_call x1, Pallas kernels, on_device(): pl.pallas_call(functools.partial(kernel, sizes), out_shape=jax.ShapeDtype...  14 us
    unnamed x1, local copies, waits for them, and re-layouts  1.47 us

profile of v4, /device:TPU:3, one launch (start us, length us, event | category | flops | bytes accessed | tf_op | source)
XLA Modules:
  0.0 15.4 jit_solution(13688032091019439327)
XLA Ops:
  0.0 14.0 %shard_map.100 = bf16[16,16,128]{2,1,0:T(8,128)(2,1)} custom-call(bf16[128,8,256]{2,1,0:T(8,128)(2,1)} %x_hbm.1, bf16[8,128]{1,0:T(8,128)(2,1)} %bitcast.9, f32[1,256]{1,0:T(1,128)} %bitcast.10, f32[1,256]{1,0:T(1,128)} %bitcast.11, bf16[32,256]{1,0:T(8,128)(2,1)} %bitcast.7, f32[1,32]{1,0:T(1,128)} %bitcast.12, bf16[32,256]{1,0:T(8,128)(2,1)} %bitcast.8, ...), custom_call_target="tpu_custom_call" | custom-call | tf_op jit(solution)/shard_map/pallas_call | solution.py:296
  14.0 1.5 %copy.12 = bf16[16,16,128]{2,1,0:T(8,128)(2,1)} copy(bf16[16,16,128]{2,1,0:T(8,128)(2,1)} %shard_map.100) | data formatting | bytes 131072
